TPU v7x, 32 devices: a whole 2x2x4 slice. The times are simulated.
32 devices in a mesh: seq: 16 (over z, y, core), head: 2 (over x).
Axes of the slice: x: 2, y: 2, z: 4, core: 2. Of those that a mesh axis runs over, the one named last changes fastest.
Arguments:
- att_q: bfloat16 [4096, 1280], P('seq', 'head'), may hold values from -150 to 150
- att_k: bfloat16 [4096, 1280], P('seq', 'head'), may hold values from -6 to 6
- att_v: bfloat16 [4096, 1280], P('seq', 'head'), may hold values from -6 to 6
- fast_q: bfloat16 [4096, 1280], P('seq', 'head'), may hold values from -6 to 6
- fast_k: bfloat16 [4096, 1280], P('seq', 'head'), may hold values from -6 to 6
- fast_v: bfloat16 [4096, 1280], P('seq', 'head'), may hold values from -6 to 6
- learn_rates: float32 [4096], P('seq'), may hold values from 0.0002 to 0.002
- w_gate: bfloat16 [640, 1280], P(None, 'head'), may hold values from -0.25 to 0.25
- w_up: bfloat16 [640, 1280], P(None, 'head'), may hold values from -0.25 to 0.25
- w_down: bfloat16 [640, 1280], P(None, 'head'), may hold values from -0.25 to 0.25
Outputs:
- attended: bfloat16 [4096, 1280], P('seq', 'head')
- fast_out: bfloat16 [4096, 1280], P('seq', 'head')
All inputs are finite; a program needn't handle non-finite values.
Results may differ from a plain program's by a relative error of at most 0.007.
The roundings to bfloat16 on the way count: a program that leaves them out, or rounds other values in their place, can miss the bound.
Values may be sent and summed in bfloat16 or wider, within the bound.
No kernel may reach another device: no remote copies, remote signals or barrier semaphores. Data moves between devices by JAX's collectives and lax.ppermute only.
A program may use at most 64 MiB of HBM per device.

v0:
```python
import functools
import math

import jax
import jax.numpy as jnp
from jax import lax
from jax.experimental import pallas as pl
from jax.experimental.pallas import tpu as pltpu
from jax.sharding import PartitionSpec as P

WINDOW = 1024
HEAD_DIM = 128
norm_eps = 1e-06
f32 = jnp.float32
bf16 = jnp.bfloat16

SMEM = pl.BlockSpec(memory_space=pltpu.SMEM)
VMEM = pl.BlockSpec(memory_space=pltpu.VMEM)
HBM = pl.BlockSpec(memory_space=pltpu.HBM)
ANY = pl.BlockSpec(memory_space=pl.ANY)
PARAMS = pltpu.CompilerParams(vmem_limit_bytes=16 << 20)


def swapped(value, bit):
    count = lax.axis_size("seq")
    return lax.ppermute(value, "seq", [(at, at ^ bit) for at in range(count)])


def kernel_call(kernel, operands, tied=(), in_specs=None, name=None, **rest):
    given = len(operands)

    def run(*refs):
        kernel(*refs[:given], *refs[given + len(tied) :])

    return pl.pallas_call(
        run, in_specs=list(in_specs) + [ANY] * len(tied), name=name, **rest
    )(*operands, *tied)


def cost(flops, moved_bytes, exps=0):
    return pl.CostEstimate(flops=flops, bytes_accessed=moved_bytes, transcendentals=exps)


def attention_kernel(
    place_ref, q_ref, own_k, own_v, back2_k, back2_v, back4_ref, pair_ref, out_ref
):
    back4_k, back4_v = back4_ref.at[0], back4_ref.at[1]
    keys = [own_k, back4_k, pair_ref.at[0, 0], back2_k, pair_ref.at[1, 0]]
    vals = [own_v, back4_v, pair_ref.at[0, 1], back2_v, pair_ref.at[1, 1]]
    rows, width = q_ref.shape
    place = place_ref[0]
    factor = HEAD_DIM ** (-0.5) * math.log2(math.e)
    q_at = lax.broadcasted_iota(jnp.int32, (rows, rows), 0)
    k_at = lax.broadcasted_iota(jnp.int32, (rows, rows), 1)
    inside = k_at <= q_at

    def attend(cols, masked):
        query = q_ref[:, cols]

        def score(at):
            return lax.dot_general(
                query, keys[at][:, cols], (((1,), (1,)), ((), ())), preferred_element_type=f32
            )

        def seen(part, back):
            return jnp.where(place >= back, part, -1e30) if masked else part

        parts = [jnp.where(inside, score(0), seen(score(1), 4))]
        parts += [seen(score(at), at - 1) for at in range(2, 5)]
        row_max = functools.reduce(
            jnp.maximum, [jnp.max(part, axis=1, keepdims=True) for part in parts]
        )
        shift = row_max * factor
        parts = [jnp.exp2(part * factor - shift) for part in parts]
        total = functools.reduce(jnp.add, [jnp.sum(e, axis=1, keepdims=True) for e in parts])
        scale = 1.0 / total
        parts = [(part * scale).astype(bf16) for part in parts]
        zero = jnp.zeros_like(parts[0])
        parts = [jnp.where(inside, parts[0], zero), jnp.where(inside, zero, parts[0])] + parts[1:]
        result = jnp.zeros((rows, HEAD_DIM), f32)
        for part, val in zip(parts, vals):
            result += jnp.dot(part, val[:, cols], preferred_element_type=f32)
        out_ref[:, cols] = result.astype(bf16)

    def every(masked):
        for head in range(width // HEAD_DIM):
            attend(slice(head * HEAD_DIM, (head + 1) * HEAD_DIM), masked)

    pl.when(place >= 4)(lambda: every(False))
    pl.when(place < 4)(lambda: every(True))


def attention(place, query, blocks, pair):
    rows, width = query.shape
    return pl.pallas_call(
        attention_kernel,
        out_shape=jax.ShapeDtypeStruct((rows, width), bf16),
        in_specs=[SMEM] + [VMEM] * 7,
        out_specs=VMEM,
        compiler_params=PARAMS,
        cost_estimate=cost(20 * rows * rows * width, 24 * rows * width, 5 * rows * rows * 5),
        name="attention",
    )(place[None], query, *blocks, pair)


def prepare_kernel(place_ref, gate_ref, up_ref, down_ref, out_ref, hold):
    hidden = gate_ref.shape[1]
    half = hidden // 2
    window = hold.shape[0]
    core = place_ref[0] % 2
    low = pl.multiple_of(core * (hidden - window), 128)
    off = pl.multiple_of(core * (half - hidden + window), 64)
    for at, ref in enumerate((gate_ref, up_ref, down_ref)):
        hold[...] = ref[:, pl.ds(low, window)].T
        out_ref[at] = hold[pl.ds(off, half), :]


def prepared(place, w_gate, w_up, w_down):
    feats, hidden = w_gate.shape
    half = hidden // 2
    window = -(-half // 128) * 128
    return pl.pallas_call(
        prepare_kernel,
        out_shape=jax.ShapeDtypeStruct((3, half, feats), bf16),
        in_specs=[SMEM] + [VMEM] * 3,
        out_specs=VMEM,
        scratch_shapes=[pltpu.VMEM((window, feats), bf16)],
        compiler_params=PARAMS,
        cost_estimate=cost(0, 9 * feats * hidden),
        name="prepare",
    )(place[None], w_gate, w_up, w_down)


def pack_kernel(key_ref, val_ref, own_ref):
    own_ref[0] = key_ref[...]
    own_ref[1] = val_ref[...]


def packed(att_k, att_v, *tied):
    return kernel_call(
        pack_kernel,
        (att_k, att_v),
        tied,
        out_shape=jax.ShapeDtypeStruct((2,) + att_k.shape, bf16),
        in_specs=[VMEM] * 2,
        out_specs=VMEM,
        compiler_params=PARAMS,
        cost_estimate=cost(0, 0),
        name="pack",
    )


def grad_kernel(
    place_ref, turned_ref, k0_ref, k1_ref, v0_ref, v1_ref, r0_ref, r1_ref,
    send_p, send_q, keep_p, keep_q, hold,
):
    def project(at, rows):
        return lax.dot_general(
            turned_ref[at], rows, (((1,), (1,)), ((), ())), preferred_element_type=f32
        )

    terms = []
    for keys, vals, rate_ref in ((k0_ref, v0_ref, r0_ref), (k1_ref, v1_ref, r1_ref)):
        rate = rate_ref[...]
        pre_gate = project(0, keys[...])
        pre_up = project(1, keys[...])
        back = rate * project(2, vals[...])
        sigmoid_v = jax.nn.sigmoid(pre_gate)
        silu = pre_gate * sigmoid_v
        slope = sigmoid_v * (1.0 + pre_gate * (1.0 - sigmoid_v))
        terms.append(
            (
                (back * pre_up * slope).astype(bf16),
                (back * silu).astype(bf16),
                (rate * silu * pre_up).astype(bf16),
            )
        )
    sources = ((k0_ref, k1_ref), (k0_ref, k1_ref), (v0_ref, v1_ref))
    for at in range(3):
        hold[at] = jnp.dot(
            terms[0][at], sources[at][0][...], preferred_element_type=f32
        ) + jnp.dot(terms[1][at], sources[at][1][...], preferred_element_type=f32)
    quart = send_p.shape[2]
    row = (place_ref[0] // 2) % 2
    for at in range(3):
        send, keep = (send_p.at[at], keep_p.at[at]) if at < 2 else (send_q.at[0], keep_q.at[0])
        for other in range(2):
            there = pl.multiple_of((2 * (1 - row) + other) * quart, 8)
            here = pl.multiple_of((2 * row + other) * quart, 8)
            send[other] = hold[at, pl.ds(there, quart), :].astype(bf16)
            keep[other] = hold[at, pl.ds(here, quart), :]


def gradients(place, turned_w, k0, k1, v0, v1, r0, r1, *tied):
    _, half, feats = turned_w.shape
    rows = k0.shape[0]
    return kernel_call(
        grad_kernel,
        (place[None], turned_w, k0, k1, v0, v1, r0, r1),
        tied,
        out_shape=[
            jax.ShapeDtypeStruct((count, 2, half // 4, feats), kind)
            for kind in (bf16, f32)
            for count in (2, 1)
        ],
        in_specs=[SMEM] + [VMEM] * 7,
        out_specs=[VMEM] * 4,
        scratch_shapes=[pltpu.VMEM((3, half, feats), f32)],
        compiler_params=PARAMS,
        cost_estimate=cost(24 * rows * half * feats, 20 * half * feats, 2 * half * rows),
        name="gradients",
    )


def stage(kernel, operands, outs, name, *tied):
    return kernel_call(
        kernel,
        (operands[0][None], *operands[1:]),
        tied,
        out_shape=[jax.ShapeDtypeStruct(shape, kind) for shape, kind in outs],
        in_specs=[SMEM] + [VMEM] * (len(operands) - 1),
        out_specs=[VMEM] * len(outs),
        compiler_params=PARAMS,
        cost_estimate=cost(0, 0),
        name=name,
    )


def halve(place_ref, keep, got, send, kept):
    row = (place_ref[0] // 4) % 2
    for at in range(keep.shape[0]):
        send[at] = (keep[at, 1 - row] + got[at, 1 - row].astype(f32)).astype(bf16)
        kept[at] = keep[at, row] + got[at, row].astype(f32)


def add(place_ref, keep, got, send, total):
    for at in range(keep.shape[0]):
        summed = keep[at] + got[at].astype(f32)
        total[at] = summed
        send[at] = summed.astype(bf16)


def window_kernel(place_ref, own_k, own_v, back_ref, out_k, out_v):
    back_k, back_v = back_ref.at[0], back_ref.at[1]
    early = (place_ref[0] // 2) % 2 == 0

    @pl.when(early)
    def _():
        out_k[...] = own_k[...]
        out_v[...] = own_v[...]

    @pl.when(jnp.logical_not(early))
    def _():
        out_k[...] = back_k[...]
        out_v[...] = back_v[...]


def renorm_kernel(place_ref, old_ref, keep_p, got_p, keep_q, got_q, part_a, part_b):
    rows = part_a.shape[1]
    units = 2 * rows
    first = 0
    if old_ref.shape[1] > units:
        quart = old_ref.shape[1] // 4
        first = (place_ref[0] // 2) % 2 * (2 * quart) + (place_ref[0] // 4) % 2 * quart
        first = pl.multiple_of(first, 16)
    for at in range(3):
        keep, got = (keep_p[at], got_p[at]) if at < 2 else (keep_q[0], got_q[0])
        old = old_ref[at, pl.ds(first, units), :].astype(f32)
        updated = old + (keep + got.astype(f32))
        old_norm = jnp.sqrt(jnp.sum(old * old, axis=1, keepdims=True))
        squares = jnp.sum(updated * updated, axis=1, keepdims=True)
        fresh = updated * (old_norm / jnp.sqrt(squares + norm_eps))
        part_a[at] = fresh[:rows].astype(bf16)
        part_b[at] = fresh[rows:].astype(bf16)


def near_kernel(
    place_ref, part_a, got_a, part_b, got_b, own_k, own_v, back2_k, back2_v, back4_ref,
    near_a, near_b, near, pair,
):
    back4_k, back4_v = back4_ref.at[0], back4_ref.at[1]
    rows = part_a.shape[1]
    for at in range(3):
        for part, got, out, low in (
            (part_a, got_a, near_a, 0),
            (part_b, got_b, near_b, 2 * rows),
        ):
            both = jnp.concatenate([part[at].astype(f32), got[at].astype(f32)], axis=0)
            out[at] = both.astype(bf16)
            near[at, low : low + 2 * rows] = both.astype(bf16)
    even = place_ref[0] % 2 == 0

    @pl.when(even)
    def _():
        pair[0, 0] = own_k[...]
        pair[0, 1] = own_v[...]
        pair[1, 0] = back2_k[...]
        pair[1, 1] = back2_v[...]

    @pl.when(jnp.logical_not(even))
    def _():
        pair[0, 0] = back2_k[...]
        pair[0, 1] = back2_v[...]
        pair[1, 0] = back4_k[...]
        pair[1, 1] = back4_v[...]


def near_rows(place, part_a, got_a, part_b, got_b, blocks):
    rows, feats = part_a.shape[1:]
    return pl.pallas_call(
        near_kernel,
        out_shape=[
            jax.ShapeDtypeStruct((3, size * rows, feats), bf16) for size in (2, 2, 4)
        ]
        + [jax.ShapeDtypeStruct((2, 2) + blocks[0].shape, bf16)],
        in_specs=[SMEM] + [VMEM] * 9,
        out_specs=[VMEM] * 4,
        compiler_params=PARAMS,
        cost_estimate=cost(0, part_a.size * 14 + blocks[0].size * 8),
        name="near",
    )(place[None], part_a, got_a, part_b, got_b, *blocks)


def fast_output(query, hold):
    gate_q = lax.dot_general(
        query, hold[0], (((1,), (1,)), ((), ())), preferred_element_type=f32
    )
    up_q = lax.dot_general(query, hold[1], (((1,), (1,)), ((), ())), preferred_element_type=f32)
    hidden_q = (gate_q * jax.nn.sigmoid(gate_q) * up_q).astype(bf16)
    return jnp.dot(hidden_q, hold[2], preferred_element_type=f32)


def first_kernel(q_ref, near, near_other, out_ref, hold):
    rows = near.shape[1]
    hold[:, :rows] = near[...]
    hold[:, rows:] = near_other[...]
    out_ref[...] = fast_output(q_ref[...], hold)


def first_half(query, near, near_other):
    rows, feats = query.shape
    units = 2 * near.shape[1]
    return pl.pallas_call(
        first_kernel,
        out_shape=jax.ShapeDtypeStruct((rows, feats), f32),
        in_specs=[VMEM] * 3,
        out_specs=VMEM,
        scratch_shapes=[pltpu.VMEM((3, units, feats), bf16)],
        compiler_params=PARAMS,
        cost_estimate=cost(6 * rows * units * feats, 12 * units * feats, units * rows),
        name="first_half",
    )(query, near, near_other)


def far_kernel(got_a, got_b, attended, half_out, far, passed, passed_half):
    del attended, half_out, passed, passed_half
    rows = got_a.shape[1]
    far[:, :rows] = got_a[...]
    far[:, rows:] = got_b[...]


def far_rows(got_a, got_b, attended, half_out):
    shape = (3, 2 * got_a.shape[1], got_a.shape[2])
    return pl.pallas_call(
        far_kernel,
        out_shape=[
            jax.ShapeDtypeStruct(shape, bf16),
            jax.ShapeDtypeStruct(attended.shape, bf16),
            jax.ShapeDtypeStruct(half_out.shape, f32),
        ],
        in_specs=[VMEM] * 2 + [ANY] * 2,
        out_specs=[VMEM, ANY, ANY],
        input_output_aliases={2: 1, 3: 2},
        compiler_params=PARAMS,
        cost_estimate=cost(0, got_a.size * 8),
        name="far",
    )(got_a, got_b, attended, half_out)


def part_kernel(q_ref, before, rows_ref, out_ref):
    out_ref[...] = (before[...] + fast_output(q_ref[...], rows_ref)).astype(out_ref.dtype)


def part_step(query, before, weights, kind, name):
    rows, feats = query.shape
    units = weights.shape[1]
    return pl.pallas_call(
        part_kernel,
        out_shape=jax.ShapeDtypeStruct((rows, feats), kind),
        in_specs=[VMEM] * 3,
        out_specs=VMEM,
        compiler_params=PARAMS,
        cost_estimate=cost(6 * rows * units * feats, 6 * units * feats, units * rows),
        name=name,
    )(query, before, weights)


def body(att_q, att_k, att_v, fast_q, fast_k, fast_v, learn_rates, w_gate, w_up, w_down):
    count = lax.axis_size("seq")
    place = lax.axis_index("seq")
    feats, hidden = w_gate.shape
    quart = hidden // 8
    later = [1 << at for at in range(3, count.bit_length() - 1)]
    own_bit = {bit: (place // bit) % 2 for bit in [2, 4] + later}

    other_k, other_v = swapped(fast_k, 1), swapped(fast_v, 1)
    other_r = swapped(learn_rates, 1)
    turned_w = prepared(place, w_gate, w_up, w_down)
    own = packed(att_k, att_v, turned_w, other_r)
    back4 = lax.ppermute(own, "seq", [(at, (at + 4) % count) for at in range(count)])
    send_p, send_q, keep_p, keep_q = gradients(
        place, turned_w, fast_k, other_k, fast_v, other_v,
        learn_rates[None, :], other_r[None, :], own,
    )
    rest = quart
    start = own_bit[2] * 2 * quart + own_bit[4] * quart
    for bit in later[:-1]:
        rest //= 2
        start += own_bit[bit] * rest
    old = turned_w
    if len(later) > 1 or quart % 16 > 0:
        old = lax.dynamic_slice_in_dim(turned_w, start, rest, 1)

    def shapes(matrices):
        return [((matrices, quart, feats), bf16), ((matrices, quart, feats), f32)]

    def scattered(send, total):
        for bit in later[:-1]:
            total = total.reshape(total.shape[0], 2, -1, feats)
            send = lax.dynamic_index_in_dim(total, 1 - own_bit[bit], 1, keepdims=False)
            total = lax.dynamic_index_in_dim(total, own_bit[bit], 1, keepdims=False)
            total = total + swapped(send.astype(bf16), bit).astype(f32)
            send = total.astype(bf16)
        return total, swapped(send, later[-1])

    got_p, got_q = swapped(send_p, 2), swapped(send_q, 2)
    send_p, keep_p = stage(halve, (place, keep_p, got_p), shapes(2), "second_p")
    got_p = swapped(send_p, 4)
    send_q, keep_q = stage(halve, (place, keep_q, got_q), shapes(1), "second_q", send_p)
    got_q = swapped(send_q, 4)
    send_p, total_p = stage(add, (place, keep_p, got_p), shapes(2), "third_p", send_q)
    windows = stage(
        window_kernel,
        (place, att_k, att_v, back4),
        [(att_k.shape, bf16)] * 2,
        "window",
        send_p,
    )
    back2_k, back2_v = (swapped(part, 2) for part in windows)
    blocks = (att_k, att_v, back2_k, back2_v, back4)
    total_p, got_p = scattered(send_p, total_p)
    send_q, total_q = stage(add, (place, keep_q, got_q), shapes(1), "third_q", send_p)
    total_q, got_q = scattered(send_q, total_q)
    part_a, part_b = stage(
        renorm_kernel,
        (place, old, total_p, got_p, total_q, got_q),
        [((3, rest // 2, feats), bf16)] * 2,
        "renorm",
    )

    for bit in reversed(later[:-1]):
        part_a = jnp.concatenate([part_a, swapped(part_a, bit)], axis=1)
        part_b = jnp.concatenate([part_b, swapped(part_b, bit)], axis=1)
    near_a, near_b, near, pair = near_rows(
        place, part_a, swapped(part_a, 4), part_b, swapped(part_b, 2), blocks
    )
    got_a, got_b = swapped(near_a, 2), swapped(near_b, 4)
    near_other = swapped(near, 1)
    pair = swapped(pair, 1)
    attended = attention(place, att_q, blocks, pair)
    half_out = first_half(fast_q, near, near_other)
    far, attended, half_out = far_rows(got_a, got_b, attended, half_out)
    half_out = part_step(fast_q, half_out, far, f32, "own_far")
    fast_out = part_step(fast_q, half_out, swapped(far, 1), bf16, "last")
    return (attended, fast_out)


def solution(mesh):
    tokens = P("seq", "head")
    weights = P(None, "head")
    return jax.shard_map(
        body,
        mesh=mesh,
        in_specs=(tokens,) * 6 + (P("seq"),) + (weights,) * 3,
        out_specs=(tokens, tokens),
        check_vma=False,
    )
```

profile of v0, /device:TPU:0, one launch (start us, length us, event | category | flops | bytes accessed | tf_op | source)
XLA Modules:
  0.0 66.6 jit_solution(9185433036714719349)
XLA Ops:
  0.6 0.5 collective-permute-start
  1.2 0.4 collective-permute-start.2
  1.7 1.1 %copy-done.3 = bf16[640,640]{1,0:T(8,128)(2,1)S(1)} copy-done((bf16[640,640]{1,0:T(8,128)(2,1)S(1)}, bf16[640,640]{1,0:T(8,128)(2,1)}, u32[]{:S(2)}) %copy-start.3) | copy-done | bytes 819224
  2.8 1.1 %copy-done.4 = bf16[640,640]{1,0:T(8,128)(2,1)S(1)} copy-done((bf16[640,640]{1,0:T(8,128)(2,1)S(1)}, bf16[640,640]{1,0:T(8,128)(2,1)}, u32[]{:S(2)}) %copy-start.4) | copy-done | bytes 819224
  4.0 1.1 %copy-done.5 = bf16[640,640]{1,0:T(8,128)(2,1)S(1)} copy-done((bf16[640,640]{1,0:T(8,128)(2,1)S(1)}, bf16[640,640]{1,0:T(8,128)(2,1)}, u32[]{:S(2)}) %copy-start.5) | copy-done | bytes 819224
  5.1 0.6 prepare.1.refs_2_.refs_1_
  5.7 0.4 copy-done
  6.2 2.7 %collective-permute-start.11 = (bf16[2,256,640]{2,1,0:T(8,128)(2,1)S(1)}, bf16[2,256,640]{2,1,0:T(8,128)(2,1)S(1)}, u32[]{:S(2)}, u32[]{:S(2)}) collective-permute-start(bf16[2,256,640]{2,1,0:T(8,128)(2,1)S(1)} %pack.1.refs_8_), channel_id=1, source_target_pairs={{0,8},{2,10},{4,12},{6,14},{8,16},{10,18},{12,20},{14,22},{16,24},... | collective-permute-start | bytes 1966088 | tf_op jit(solution)/shard_map/ppermute | solution.py:410
  9.0 2.4 %gradients.1 = (bf16[2,2,80,640]{3,2,1,0:T(8,128)(2,1)S(1)}, bf16[1,2,80,640]{3,2,1,0:T(8,128)(2,1)S(1)}, f32[2,2,80,640]{3,2,1,0:T(8,128)S(1)}, f32[1,2,80,640]{3,2,1,0:T(8,128)S(1)}) custom-call(s32[1]{0:T(128)} %bitcast.place_ref.refs_0_, bf16[3,320,640]{2,1,0:T(8,128)(2,1)S(1)} %prepare.1.refs_2_.refs_1_, bf16[256,640]{1,0:T(8,128)(2,1)S(1)} %copy-done.7, ...), custom_call_target="tpu_custom_call" | custom-call | flops 1258291200 | bytes 4096000 | tf_op jit(solution)/shard_map/gradients/pallas_call | solution.py:35
  11.4 1.6 %collective-permute-start.3 = (bf16[2,2,80,640]{3,2,1,0:T(8,128)(2,1)S(1)}, bf16[2,2,80,640]{3,2,1,0:T(8,128)(2,1)S(1)}, u32[]{:S(2)}, u32[]{:S(2)}) collective-permute-start(bf16[2,2,80,640]{3,2,1,0:T(8,128)(2,1)S(1)} %get-tuple-element.26), channel_id=1, source_target_pairs={{0,4},{2,6},{4,0},{6,2},{8,12},{10,14},{12,8},{14,10},{16,20},{18,... | collective-permute-start | bytes 1228808 | tf_op jit(solution)/shard_map/ppermute | solution.py:26
  13.0 0.5 collective-permute-start.5
  13.5 10.3 %collective-permute-done.3.refs_2_ = bf16[2,2,80,640]{3,2,1,0:T(8,128)(2,1)S(1)} collective-permute-done((bf16[2,2,80,640]{3,2,1,0:T(8,128)(2,1)S(1)}, bf16[2,2,80,640]{3,2,1,0:T(8,128)(2,1)S(1)}, u32[]{:S(2)}, u32[]{:S(2)}) %collective-permute-start.3) | collective-permute-done | bytes 409632 | tf_op jit(solution)/shard_map/ppermute | solution.py:26
  23.8 1.7 %collective-permute-start.4 = (bf16[2,80,640]{2,1,0:T(8,128)(2,1)S(1)}, bf16[2,80,640]{2,1,0:T(8,128)(2,1)S(1)}, u32[]{:S(2)}, u32[]{:S(2)}) collective-permute-start(bf16[2,80,640]{2,1,0:T(8,128)(2,1)S(1)} %get-tuple-element.28.refs_3_), channel_id=1, source_target_pairs={{0,8},{2,10},{4,12},{6,14},{8,0},{10,2},{12,4},{14,6},{16,24},{18,... | collective-permute-start | bytes 614408 | tf_op jit(solution)/shard_map/ppermute | solution.py:26
  25.5 1.9 %collective-permute-done.5.refs_2_ = bf16[1,2,80,640]{3,2,1,0:T(8,128)(2,1)S(1)} collective-permute-done((bf16[1,2,80,640]{3,2,1,0:T(8,128)(2,1)S(1)}, bf16[1,2,80,640]{3,2,1,0:T(8,128)(2,1)S(1)}, u32[]{:S(2)}, u32[]{:S(2)}) %collective-permute-start.5) | collective-permute-done | bytes 204832 | tf_op jit(solution)/shard_map/ppermute | solution.py:26
  27.4 1.6 %collective-permute-start.7 = (bf16[1,80,640]{2,1,0:T(8,128)(2,1)S(1)}, bf16[1,80,640]{2,1,0:T(8,128)(2,1)S(1)}, u32[]{:S(2)}, u32[]{:S(2)}) collective-permute-start(bf16[1,80,640]{2,1,0:T(8,128)(2,1)S(1)} %get-tuple-element.31.refs_3_), channel_id=1, source_target_pairs={{0,8},{2,10},{4,12},{6,14},{8,0},{10,2},{12,4},{14,6},{16,24},{18,... | collective-permute-start | bytes 307208 | tf_op jit(solution)/shard_map/ppermute | solution.py:26
  29.1 2.7 %collective-permute-done.4.refs_2_ = bf16[2,80,640]{2,1,0:T(8,128)(2,1)S(1)} collective-permute-done((bf16[2,80,640]{2,1,0:T(8,128)(2,1)S(1)}, bf16[2,80,640]{2,1,0:T(8,128)(2,1)S(1)}, u32[]{:S(2)}, u32[]{:S(2)}) %collective-permute-start.4) | collective-permute-done | bytes 204832 | tf_op jit(solution)/shard_map/ppermute | solution.py:26
  31.8 0.7 %collective-permute-start.6 = (bf16[2,80,640]{2,1,0:T(8,128)(2,1)S(1)}, bf16[2,80,640]{2,1,0:T(8,128)(2,1)S(1)}, u32[]{:S(2)}, u32[]{:S(2)}) collective-permute-start(bf16[2,80,640]{2,1,0:T(8,128)(2,1)S(1)} %get-tuple-element.33.refs_3_.refs_4_), channel_id=1, source_target_pairs={{0,16},{2,18},{4,20},{6,22},{8,24},{10,26},{12,28},{14,30},{16,0},... | collective-permute-start | bytes 614408 | tf_op jit(solution)/shard_map/ppermute | solution.py:26
  32.6 1.6 %collective-permute-start.12 = (bf16[256,640]{1,0:T(8,128)(2,1)S(1)}, bf16[256,640]{1,0:T(8,128)(2,1)S(1)}, u32[]{:S(2)}, u32[]{:S(2)}) collective-permute-start(bf16[256,640]{1,0:T(8,128)(2,1)S(1)} %get-tuple-element.39), channel_id=1, source_target_pairs={{0,4},{2,6},{4,0},{6,2},{8,12},{10,14},{12,8},{14,10},{16,20},{18,... | collective-permute-start | bytes 983048 | tf_op jit(solution)/shard_map/ppermute | solution.py:26
  34.3 0.5 collective-permute-start.13
  34.8 2.3 %collective-permute-start.8 = (bf16[1,80,640]{2,1,0:T(8,128)(2,1)S(1)}, bf16[1,80,640]{2,1,0:T(8,128)(2,1)S(1)}, u32[]{:S(2)}, u32[]{:S(2)}) collective-permute-start(bf16[1,80,640]{2,1,0:T(8,128)(2,1)S(1)} %get-tuple-element.36), channel_id=1, source_target_pairs={{0,16},{2,18},{4,20},{6,22},{8,24},{10,26},{12,28},{14,30},{16,0},... | collective-permute-start | bytes 307208 | tf_op jit(solution)/shard_map/ppermute | solution.py:26
  37.1 8.9 %collective-permute-done.8.refs_5_ = bf16[1,80,640]{2,1,0:T(8,128)(2,1)S(1)} collective-permute-done((bf16[1,80,640]{2,1,0:T(8,128)(2,1)S(1)}, bf16[1,80,640]{2,1,0:T(8,128)(2,1)S(1)}, u32[]{:S(2)}, u32[]{:S(2)}) %collective-permute-start.8) | collective-permute-done | bytes 102432 | tf_op jit(solution)/shard_map/ppermute | solution.py:26
  46.4 1.6 %collective-permute-start.10 = (bf16[3,40,640]{2,1,0:T(8,128)(2,1)S(1)}, bf16[3,40,640]{2,1,0:T(8,128)(2,1)S(1)}, u32[]{:S(2)}, u32[]{:S(2)}) collective-permute-start(bf16[3,40,640]{2,1,0:T(8,128)(2,1)S(1)} %get-tuple-element.38.part_b), channel_id=1, source_target_pairs={{0,4},{2,6},{4,0},{6,2},{8,12},{10,14},{12,8},{14,10},{16,20},{18,... | collective-permute-start | bytes 460808 | tf_op jit(solution)/shard_map/ppermute | solution.py:26
  48.0 3.6 %collective-permute-done.9.got_a = bf16[3,40,640]{2,1,0:T(8,128)(2,1)S(1)} collective-permute-done((bf16[3,40,640]{2,1,0:T(8,128)(2,1)S(1)}, bf16[3,40,640]{2,1,0:T(8,128)(2,1)S(1)}, u32[]{:S(2)}, u32[]{:S(2)}) %collective-permute-start.9) | collective-permute-done | bytes 153632 | tf_op jit(solution)/shard_map/ppermute | solution.py:26
  51.9 0.5 collective-permute-start.17
  52.4 1.5 %collective-permute-start.14 = (bf16[3,80,640]{2,1,0:T(8,128)(2,1)S(1)}, bf16[3,80,640]{2,1,0:T(8,128)(2,1)S(1)}, u32[]{:S(2)}, u32[]{:S(2)}) collective-permute-start(bf16[3,80,640]{2,1,0:T(8,128)(2,1)S(1)} %get-tuple-element.41), channel_id=1, source_target_pairs={{0,4},{2,6},{4,0},{6,2},{8,12},{10,14},{12,8},{14,10},{16,20},{18,... | collective-permute-start | bytes 921608 | tf_op jit(solution)/shard_map/ppermute | solution.py:26
  53.9 1.9 %collective-permute-start.15 = (bf16[3,80,640]{2,1,0:T(8,128)(2,1)S(1)}, bf16[3,80,640]{2,1,0:T(8,128)(2,1)S(1)}, u32[]{:S(2)}, u32[]{:S(2)}) collective-permute-start(bf16[3,80,640]{2,1,0:T(8,128)(2,1)S(1)} %get-tuple-element.42), channel_id=1, source_target_pairs={{0,8},{2,10},{4,12},{6,14},{8,0},{10,2},{12,4},{14,6},{16,24},{18,... | collective-permute-start | bytes 921608 | tf_op jit(solution)/shard_map/ppermute | solution.py:26
  55.9 0.8 %first_half.1.half_out = f32[256,640]{1,0:T(8,128)S(1)} custom-call(bf16[256,640]{1,0:T(8,128)(2,1)S(1)} %copy-done.2, bf16[3,160,640]{2,1,0:T(8,128)(2,1)S(1)} %get-tuple-element.44.near, bf16[3,160,640]{2,1,0:T(8,128)(2,1)S(1)} %collective-permute-done.17.near_other), custom_call_target="tpu_custom_call" | custom-call | flops 314572800 | bytes 2457600 | tf_op jit(solution)/shard_map/first_half/pallas_call | solution.py:343
  56.8 4.7 %attention.1.attended = bf16[256,640]{1,0:T(8,128)(2,1)} custom-call(s32[1]{0:T(128)} %bitcast.place_ref.refs_0_, bf16[256,640]{1,0:T(8,128)(2,1)S(1)} %copy-done.6, bf16[256,640]{1,0:T(8,128)(2,1)S(1)} %copy-done, bf16[256,640]{1,0:T(8,128)(2,1)S(1)} %copy-done.1, bf16[256,640]{1,0:T(8,128)(2,1)S(1)} %collective-permute-done.12.back2_k, ...), custom_call_target="tpu_custom_call" | custom-call | flops 838860800 | bytes 3932160 | tf_op jit(solution)/shard_map/attention/pallas_call | solution.py:95
  61.7 1.4 %collective-permute-done.15.got_b = bf16[3,80,640]{2,1,0:T(8,128)(2,1)S(1)} collective-permute-done((bf16[3,80,640]{2,1,0:T(8,128)(2,1)S(1)}, bf16[3,80,640]{2,1,0:T(8,128)(2,1)S(1)}, u32[]{:S(2)}, u32[]{:S(2)}) %collective-permute-start.15) | collective-permute-done | bytes 307232 | tf_op jit(solution)/shard_map/ppermute | solution.py:26
  63.3 0.6 own_far.1.before
  63.9 1.4 %collective-permute-done.18.rows_ref = bf16[3,160,640]{2,1,0:T(8,128)(2,1)S(1)} collective-permute-done((bf16[3,160,640]{2,1,0:T(8,128)(2,1)S(1)}, bf16[3,160,640]{2,1,0:T(8,128)(2,1)S(1)}, u32[]{:S(2)}, u32[]{:S(2)}) %collective-permute-start.18) | collective-permute-done | bytes 614432 | tf_op jit(solution)/shard_map/ppermute | solution.py:26
  65.3 1.3 %last.1 = bf16[256,640]{1,0:T(8,128)(2,1)} custom-call(bf16[256,640]{1,0:T(8,128)(2,1)S(1)} %copy-done.2, f32[256,640]{1,0:T(8,128)S(1)} %own_far.1.before, bf16[3,160,640]{2,1,0:T(8,128)(2,1)S(1)} %collective-permute-done.18.rows_ref), custom_call_target="tpu_custom_call" | custom-call | flops 157286400 | bytes 614400 | tf_op jit(solution)/shard_map/last/pallas_call | solution.py:387
  (41 shorter events, 1.6 us)
Async XLA Ops:
  0.6 8.3 %collective-permute-start = (bf16[256,640]{1,0:T(8,128)(2,1)}, bf16[256,640]{1,0:T(8,128)(2,1)S(1)}, u32[]{:S(2)}, u32[]{:S(2)}) collective-permute-start(bf16[256,640]{1,0:T(8,128)(2,1)} %refs_2_.2), channel_id=1, source_target_pairs={{0,2},{2,0},{4,6},{6,4},{8,10},{10,8},{12,14},{14,12},{16,18},{18,... | collective-permute-start | bytes 983048 | tf_op jit(solution)/shard_map/ppermute | solution.py:26
  1.1 7.8 %collective-permute-start.1 = (bf16[256,640]{1,0:T(8,128)(2,1)}, bf16[256,640]{1,0:T(8,128)(2,1)S(1)}, u32[]{:S(2)}, u32[]{:S(2)}) collective-permute-start(bf16[256,640]{1,0:T(8,128)(2,1)} %refs_4_.1), channel_id=1, source_target_pairs={{0,2},{2,0},{4,6},{6,4},{8,10},{10,8},{12,14},{14,12},{16,18},{18,... | collective-permute-start | bytes 983048 | tf_op jit(solution)/shard_map/ppermute | solution.py:26
  1.2 4.5 %collective-permute-start.2 = (f32[256]{0:T(256)}, f32[256]{0:T(256)S(1)}, u32[]{:S(2)}, u32[]{:S(2)}) collective-permute-start(f32[256]{0:T(256)} %param.16), channel_id=1, source_target_pairs={{0,2},{2,0},{4,6},{6,4},{8,10},{10,8},{12,14},{14,12},{16,18},{18,... | collective-permute-start | bytes 3080 | tf_op jit(solution)/shard_map/ppermute | solution.py:26
  1.7 1.1 %copy-start.3 = (bf16[640,640]{1,0:T(8,128)(2,1)S(1)}, bf16[640,640]{1,0:T(8,128)(2,1)}, u32[]{:S(2)}) copy-start(bf16[640,640]{1,0:T(8,128)(2,1)} %gate_ref.1) | copy-start | bytes 2457604
  2.8 1.1 %copy-start.4 = (bf16[640,640]{1,0:T(8,128)(2,1)S(1)}, bf16[640,640]{1,0:T(8,128)(2,1)}, u32[]{:S(2)}) copy-start(bf16[640,640]{1,0:T(8,128)(2,1)} %up_ref.1) | copy-start | bytes 2457604
  4.0 1.1 %copy-start.5 = (bf16[640,640]{1,0:T(8,128)(2,1)S(1)}, bf16[640,640]{1,0:T(8,128)(2,1)}, u32[]{:S(2)}) copy-start(bf16[640,640]{1,0:T(8,128)(2,1)} %down_ref.1) | copy-start | bytes 2457604
  5.1 1.0 %copy-start = (bf16[256,640]{1,0:T(8,128)(2,1)S(1)}, bf16[256,640]{1,0:T(8,128)(2,1)}, u32[]{:S(2)}) copy-start(bf16[256,640]{1,0:T(8,128)(2,1)} %own_k.3) | copy-start | bytes 983044
  5.1 1.1 %copy-start.1 = (bf16[256,640]{1,0:T(8,128)(2,1)S(1)}, bf16[256,640]{1,0:T(8,128)(2,1)}, u32[]{:S(2)}) copy-start(bf16[256,640]{1,0:T(8,128)(2,1)} %own_v.3) | copy-start | bytes 983044
  5.7 3.3 %copy-start.7 = (bf16[256,640]{1,0:T(8,128)(2,1)S(1)}, bf16[256,640]{1,0:T(8,128)(2,1)}, u32[]{:S(2)}) copy-start(bf16[256,640]{1,0:T(8,128)(2,1)} %refs_2_.2) | copy-start | bytes 983044
  5.7 3.3 %copy-start.8 = (bf16[256,640]{1,0:T(8,128)(2,1)S(1)}, bf16[256,640]{1,0:T(8,128)(2,1)}, u32[]{:S(2)}) copy-start(bf16[256,640]{1,0:T(8,128)(2,1)} %refs_4_.1) | copy-start | bytes 983044
  5.7 3.3 %copy-start.9 = (f32[256]{0:T(256)S(1)}, f32[256]{0:T(256)}, u32[]{:S(2)}) copy-start(f32[256]{0:T(256)} %param.16) | copy-start | bytes 3076
  6.2 26.4 %collective-permute-start.11 = (bf16[2,256,640]{2,1,0:T(8,128)(2,1)S(1)}, bf16[2,256,640]{2,1,0:T(8,128)(2,1)S(1)}, u32[]{:S(2)}, u32[]{:S(2)}) collective-permute-start(bf16[2,256,640]{2,1,0:T(8,128)(2,1)S(1)} %pack.1.refs_8_), channel_id=1, source_target_pairs={{0,8},{2,10},{4,12},{6,14},{8,16},{10,18},{12,20},{14,22},{16,24},... | collective-permute-start | bytes 1966088 | tf_op jit(solution)/shard_map/ppermute | solution.py:410
  11.4 12.4 %collective-permute-start.3 = (bf16[2,2,80,640]{3,2,1,0:T(8,128)(2,1)S(1)}, bf16[2,2,80,640]{3,2,1,0:T(8,128)(2,1)S(1)}, u32[]{:S(2)}, u32[]{:S(2)}) collective-permute-start(bf16[2,2,80,640]{3,2,1,0:T(8,128)(2,1)S(1)} %get-tuple-element.26), channel_id=1, source_target_pairs={{0,4},{2,6},{4,0},{6,2},{8,12},{10,14},{12,8},{14,10},{16,20},{18,... | collective-permute-start | bytes 1228808 | tf_op jit(solution)/shard_map/ppermute | solution.py:26
  13.0 14.4 %collective-permute-start.5 = (bf16[1,2,80,640]{3,2,1,0:T(8,128)(2,1)S(1)}, bf16[1,2,80,640]{3,2,1,0:T(8,128)(2,1)S(1)}, u32[]{:S(2)}, u32[]{:S(2)}) collective-permute-start(bf16[1,2,80,640]{3,2,1,0:T(8,128)(2,1)S(1)} %get-tuple-element.30), channel_id=1, source_target_pairs={{0,4},{2,6},{4,0},{6,2},{8,12},{10,14},{12,8},{14,10},{16,20},{18,... | collective-permute-start | bytes 614408 | tf_op jit(solution)/shard_map/ppermute | solution.py:26
  23.8 7.9 %collective-permute-start.4 = (bf16[2,80,640]{2,1,0:T(8,128)(2,1)S(1)}, bf16[2,80,640]{2,1,0:T(8,128)(2,1)S(1)}, u32[]{:S(2)}, u32[]{:S(2)}) collective-permute-start(bf16[2,80,640]{2,1,0:T(8,128)(2,1)S(1)} %get-tuple-element.28.refs_3_), channel_id=1, source_target_pairs={{0,8},{2,10},{4,12},{6,14},{8,0},{10,2},{12,4},{14,6},{16,24},{18,... | collective-permute-start | bytes 614408 | tf_op jit(solution)/shard_map/ppermute | solution.py:26
  27.4 7.3 %collective-permute-start.7 = (bf16[1,80,640]{2,1,0:T(8,128)(2,1)S(1)}, bf16[1,80,640]{2,1,0:T(8,128)(2,1)S(1)}, u32[]{:S(2)}, u32[]{:S(2)}) collective-permute-start(bf16[1,80,640]{2,1,0:T(8,128)(2,1)S(1)} %get-tuple-element.31.refs_3_), channel_id=1, source_target_pairs={{0,8},{2,10},{4,12},{6,14},{8,0},{10,2},{12,4},{14,6},{16,24},{18,... | collective-permute-start | bytes 307208 | tf_op jit(solution)/shard_map/ppermute | solution.py:26
  31.8 14.1 %collective-permute-start.6 = (bf16[2,80,640]{2,1,0:T(8,128)(2,1)S(1)}, bf16[2,80,640]{2,1,0:T(8,128)(2,1)S(1)}, u32[]{:S(2)}, u32[]{:S(2)}) collective-permute-start(bf16[2,80,640]{2,1,0:T(8,128)(2,1)S(1)} %get-tuple-element.33.refs_3_.refs_4_), channel_id=1, source_target_pairs={{0,16},{2,18},{4,20},{6,22},{8,24},{10,26},{12,28},{14,30},{16,0},... | collective-permute-start | bytes 614408 | tf_op jit(solution)/shard_map/ppermute | solution.py:26
  32.6 15.3 %collective-permute-start.12 = (bf16[256,640]{1,0:T(8,128)(2,1)S(1)}, bf16[256,640]{1,0:T(8,128)(2,1)S(1)}, u32[]{:S(2)}, u32[]{:S(2)}) collective-permute-start(bf16[256,640]{1,0:T(8,128)(2,1)S(1)} %get-tuple-element.39), channel_id=1, source_target_pairs={{0,4},{2,6},{4,0},{6,2},{8,12},{10,14},{12,8},{14,10},{16,20},{18,... | collective-permute-start | bytes 983048 | tf_op jit(solution)/shard_map/ppermute | solution.py:26
  34.3 13.7 %collective-permute-start.13 = (bf16[256,640]{1,0:T(8,128)(2,1)S(1)}, bf16[256,640]{1,0:T(8,128)(2,1)S(1)}, u32[]{:S(2)}, u32[]{:S(2)}) collective-permute-start(bf16[256,640]{1,0:T(8,128)(2,1)S(1)} %get-tuple-element.40), channel_id=1, source_target_pairs={{0,4},{2,6},{4,0},{6,2},{8,12},{10,14},{12,8},{14,10},{16,20},{18,... | collective-permute-start | bytes 983048 | tf_op jit(solution)/shard_map/ppermute | solution.py:26
  34.8 11.2 %collective-permute-start.8 = (bf16[1,80,640]{2,1,0:T(8,128)(2,1)S(1)}, bf16[1,80,640]{2,1,0:T(8,128)(2,1)S(1)}, u32[]{:S(2)}, u32[]{:S(2)}) collective-permute-start(bf16[1,80,640]{2,1,0:T(8,128)(2,1)S(1)} %get-tuple-element.36), channel_id=1, source_target_pairs={{0,16},{2,18},{4,20},{6,22},{8,24},{10,26},{12,28},{14,30},{16,0},... | collective-permute-start | bytes 307208 | tf_op jit(solution)/shard_map/ppermute | solution.py:26
  46.3 9.6 %copy-start.2 = (bf16[256,640]{1,0:T(8,128)(2,1)S(1)}, bf16[256,640]{1,0:T(8,128)(2,1)}, u32[]{:S(2)}) copy-start(bf16[256,640]{1,0:T(8,128)(2,1)} %q_ref.7) | copy-start | bytes 983044
  46.3 5.3 %collective-permute-start.9 = (bf16[3,40,640]{2,1,0:T(8,128)(2,1)S(1)}, bf16[3,40,640]{2,1,0:T(8,128)(2,1)S(1)}, u32[]{:S(2)}, u32[]{:S(2)}) collective-permute-start(bf16[3,40,640]{2,1,0:T(8,128)(2,1)S(1)} %get-tuple-element.37.part_a), channel_id=1, source_target_pairs={{0,8},{2,10},{4,12},{6,14},{8,0},{10,2},{12,4},{14,6},{16,24},{18,... | collective-permute-start | bytes 460808 | tf_op jit(solution)/shard_map/ppermute | solution.py:26
  46.4 5.3 %collective-permute-start.10 = (bf16[3,40,640]{2,1,0:T(8,128)(2,1)S(1)}, bf16[3,40,640]{2,1,0:T(8,128)(2,1)S(1)}, u32[]{:S(2)}, u32[]{:S(2)}) collective-permute-start(bf16[3,40,640]{2,1,0:T(8,128)(2,1)S(1)} %get-tuple-element.38.part_b), channel_id=1, source_target_pairs={{0,4},{2,6},{4,0},{6,2},{8,12},{10,14},{12,8},{14,10},{16,20},{18,... | collective-permute-start | bytes 460808 | tf_op jit(solution)/shard_map/ppermute | solution.py:26
  51.8 4.9 %copy-start.6 = (bf16[256,640]{1,0:T(8,128)(2,1)S(1)}, bf16[256,640]{1,0:T(8,128)(2,1)}, u32[]{:S(2)}) copy-start(bf16[256,640]{1,0:T(8,128)(2,1)} %q_ref.4) | copy-start | bytes 983044
  51.8 4.9 %collective-permute-start.16 = (bf16[2,2,256,640]{3,2,1,0:T(8,128)(2,1)S(1)}, bf16[2,2,256,640]{3,2,1,0:T(8,128)(2,1)S(1)}, u32[]{:S(2)}, u32[]{:S(2)}) collective-permute-start(bf16[2,2,256,640]{3,2,1,0:T(8,128)(2,1)S(1)} %get-tuple-element.43), channel_id=1, source_target_pairs={{0,2},{2,0},{4,6},{6,4},{8,10},{10,8},{12,14},{14,12},{16,18},{18,... | collective-permute-start | bytes 3932168 | tf_op jit(solution)/shard_map/ppermute | solution.py:26
  51.9 4.0 %collective-permute-start.17 = (bf16[3,160,640]{2,1,0:T(8,128)(2,1)S(1)}, bf16[3,160,640]{2,1,0:T(8,128)(2,1)S(1)}, u32[]{:S(2)}, u32[]{:S(2)}) collective-permute-start(bf16[3,160,640]{2,1,0:T(8,128)(2,1)S(1)} %get-tuple-element.44.near), channel_id=1, source_target_pairs={{0,2},{2,0},{4,6},{6,4},{8,10},{10,8},{12,14},{14,12},{16,18},{18,... | collective-permute-start | bytes 1843208 | tf_op jit(solution)/shard_map/ppermute | solution.py:26
  52.4 9.3 %collective-permute-start.14 = (bf16[3,80,640]{2,1,0:T(8,128)(2,1)S(1)}, bf16[3,80,640]{2,1,0:T(8,128)(2,1)S(1)}, u32[]{:S(2)}, u32[]{:S(2)}) collective-permute-start(bf16[3,80,640]{2,1,0:T(8,128)(2,1)S(1)} %get-tuple-element.41), channel_id=1, source_target_pairs={{0,4},{2,6},{4,0},{6,2},{8,12},{10,14},{12,8},{14,10},{16,20},{18,... | collective-permute-start | bytes 921608 | tf_op jit(solution)/shard_map/ppermute | solution.py:26
  53.9 9.2 %collective-permute-start.15 = (bf16[3,80,640]{2,1,0:T(8,128)(2,1)S(1)}, bf16[3,80,640]{2,1,0:T(8,128)(2,1)S(1)}, u32[]{:S(2)}, u32[]{:S(2)}) collective-permute-start(bf16[3,80,640]{2,1,0:T(8,128)(2,1)S(1)} %get-tuple-element.42), channel_id=1, source_target_pairs={{0,8},{2,10},{4,12},{6,14},{8,0},{10,2},{12,4},{14,6},{16,24},{18,... | collective-permute-start | bytes 921608 | tf_op jit(solution)/shard_map/ppermute | solution.py:26
  63.2 2.1 %collective-permute-start.18 = (bf16[3,160,640]{2,1,0:T(8,128)(2,1)S(1)}, bf16[3,160,640]{2,1,0:T(8,128)(2,1)S(1)}, u32[]{:S(2)}, u32[]{:S(2)}) collective-permute-start(bf16[3,160,640]{2,1,0:T(8,128)(2,1)S(1)} %get-tuple-element.47.rows_ref), channel_id=1, source_target_pairs={{0,2},{2,0},{4,6},{6,4},{8,10},{10,8},{12,14},{14,12},{16,18},{18,... | collective-permute-start | bytes 1843208 | tf_op jit(solution)/shard_map/ppermute | solution.py:26
where the time goes:
time: 66.9 us; the launch traced here: 66.6 us
  waiting for transfers between devices  30.5 us (46%)
  starting transfers between devices  20 us (30%)
  Pallas kernels  11.3 us (17%)
  local copies, waits for them, and re-layouts  3.92 us (6%)
  between operations  0.83 us (1%)
    ppermute x18, waiting for transfers between devices, swapped(): return lax.ppermute(value, 'seq', [(at, at ^ bit) for at in range(count)])  30.5 us
    ppermute x18, starting transfers between devices, swapped(): return lax.ppermute(value, 'seq', [(at, at ^ bit) for at in range(count)])  17.3 us
    pallas_call x1, Pallas kernels, attention(): pl.pallas_call(attention_kernel, out_shape=jax.ShapeDtypeStruct((rows, wi...  4.74 us
    unnamed x20, local copies, waits for them, and re-layouts  3.92 us
    pallas_call x8, Pallas kernels, kernel_call(): pl.pallas_call(run, in_specs=list(in_specs) + [ANY] * len(tied), name=nam...  3.03 us
    ppermute x1, starting transfers between devices, body(): lax.ppermute(own, 'seq', [(at, (at + 4) % count) for at in range(count)])  2.7 us
    pallas_call x2, Pallas kernels, part_step(): pl.pallas_call(part_kernel, out_shape=jax.ShapeDtypeStruct((rows, feats),...  1.9 us
  transfers between devices with their start and end apart: 19, of which 9 were waited for; matrix products, arithmetic and copies ran while one was open for 0% of the time, Pallas kernels for 15%

commit v1 on v0

--- a/solution.py
+++ b/solution.py
@@ -406,7 +406,7 @@
     other_k, other_v = swapped(fast_k, 1), swapped(fast_v, 1)
     other_r = swapped(learn_rates, 1)
     turned_w = prepared(place, w_gate, w_up, w_down)
-    own = packed(att_k, att_v, turned_w, other_r)
+    own = packed(att_k, att_v, other_r)
     back4 = lax.ppermute(own, "seq", [(at, (at + 4) % count) for at in range(count)])
     send_p, send_q, keep_p, keep_q = gradients(
         place, turned_w, fast_k, other_k, fast_v, other_v,

time: 66.9 us -> 66.9 us (level)
  no operation moved by 1% of the time
where the time goes in v1:
time: 66.9 us; the launch traced here: 66.6 us
  waiting for transfers between devices  30.5 us (46%)
  starting transfers between devices  20 us (30%)
  Pallas kernels  11.3 us (17%)
  local copies, waits for them, and re-layouts  3.92 us (6%)
  between operations  0.83 us (1%)
    ppermute x18, waiting for transfers between devices, swapped(): return lax.ppermute(value, 'seq', [(at, at ^ bit) for at in range(count)])  30.5 us
    ppermute x18, starting transfers between devices, swapped(): return lax.ppermute(value, 'seq', [(at, at ^ bit) for at in range(count)])  17.3 us
    pallas_call x1, Pallas kernels, attention(): pl.pallas_call(attention_kernel, out_shape=jax.ShapeDtypeStruct((rows, wi...  4.74 us
    unnamed x20, local copies, waits for them, and re-layouts  3.92 us
    pallas_call x8, Pallas kernels, kernel_call(): pl.pallas_call(run, in_specs=list(in_specs) + [ANY] * len(tied), name=nam...  3.04 us
    ppermute x1, starting transfers between devices, body(): lax.ppermute(own, 'seq', [(at, (at + 4) % count) for at in range(count)])  2.7 us
    pallas_call x2, Pallas kernels, part_step(): pl.pallas_call(part_kernel, out_shape=jax.ShapeDtypeStruct((rows, feats),...  1.9 us
  transfers between devices with their start and end apart: 19, of which 9 were waited for; matrix products, arithmetic and copies ran while one was open for 0% of the time, Pallas kernels for 15%

profile of v1, /device:TPU:0, one launch (start us, length us, event | category | flops | bytes accessed | tf_op | source)
XLA Modules:
  0.0 66.6 jit_solution(12771214811351055428)
XLA Ops:
  0.6 0.5 collective-permute-start
  1.2 0.4 collective-permute-start.2
  1.7 1.1 %copy-done.3 = bf16[640,640]{1,0:T(8,128)(2,1)S(1)} copy-done((bf16[640,640]{1,0:T(8,128)(2,1)S(1)}, bf16[640,640]{1,0:T(8,128)(2,1)}, u32[]{:S(2)}) %copy-start.3) | copy-done | bytes 819224
  2.8 1.1 %copy-done.4 = bf16[640,640]{1,0:T(8,128)(2,1)S(1)} copy-done((bf16[640,640]{1,0:T(8,128)(2,1)S(1)}, bf16[640,640]{1,0:T(8,128)(2,1)}, u32[]{:S(2)}) %copy-start.4) | copy-done | bytes 819224
  4.0 1.1 %copy-done.5 = bf16[640,640]{1,0:T(8,128)(2,1)S(1)} copy-done((bf16[640,640]{1,0:T(8,128)(2,1)S(1)}, bf16[640,640]{1,0:T(8,128)(2,1)}, u32[]{:S(2)}) %copy-start.5) | copy-done | bytes 819224
  5.1 0.6 prepare.1.refs_1_
  5.7 0.4 copy-done
  6.2 2.7 %collective-permute-start.11 = (bf16[2,256,640]{2,1,0:T(8,128)(2,1)S(1)}, bf16[2,256,640]{2,1,0:T(8,128)(2,1)S(1)}, u32[]{:S(2)}, u32[]{:S(2)}) collective-permute-start(bf16[2,256,640]{2,1,0:T(8,128)(2,1)S(1)} %pack.1.refs_8_), channel_id=1, source_target_pairs={{0,8},{2,10},{4,12},{6,14},{8,16},{10,18},{12,20},{14,22},{16,24},... | collective-permute-start | bytes 1966088 | tf_op jit(solution)/shard_map/ppermute | solution.py:410
  9.0 2.4 %gradients.1 = (bf16[2,2,80,640]{3,2,1,0:T(8,128)(2,1)S(1)}, bf16[1,2,80,640]{3,2,1,0:T(8,128)(2,1)S(1)}, f32[2,2,80,640]{3,2,1,0:T(8,128)S(1)}, f32[1,2,80,640]{3,2,1,0:T(8,128)S(1)}) custom-call(s32[1]{0:T(128)} %bitcast.place_ref.refs_0_, bf16[3,320,640]{2,1,0:T(8,128)(2,1)S(1)} %prepare.1.refs_1_, bf16[256,640]{1,0:T(8,128)(2,1)S(1)} %copy-done.7, ...), custom_call_target="tpu_custom_call" | custom-call | flops 1258291200 | bytes 4096000 | tf_op jit(solution)/shard_map/gradients/pallas_call | solution.py:35
  11.4 1.6 %collective-permute-start.3 = (bf16[2,2,80,640]{3,2,1,0:T(8,128)(2,1)S(1)}, bf16[2,2,80,640]{3,2,1,0:T(8,128)(2,1)S(1)}, u32[]{:S(2)}, u32[]{:S(2)}) collective-permute-start(bf16[2,2,80,640]{3,2,1,0:T(8,128)(2,1)S(1)} %get-tuple-element.26), channel_id=1, source_target_pairs={{0,4},{2,6},{4,0},{6,2},{8,12},{10,14},{12,8},{14,10},{16,20},{18,... | collective-permute-start | bytes 1228808 | tf_op jit(solution)/shard_map/ppermute | solution.py:26
  13.0 0.5 collective-permute-start.5
  13.5 10.3 %collective-permute-done.3.refs_2_ = bf16[2,2,80,640]{3,2,1,0:T(8,128)(2,1)S(1)} collective-permute-done((bf16[2,2,80,640]{3,2,1,0:T(8,128)(2,1)S(1)}, bf16[2,2,80,640]{3,2,1,0:T(8,128)(2,1)S(1)}, u32[]{:S(2)}, u32[]{:S(2)}) %collective-permute-start.3) | collective-permute-done | bytes 409632 | tf_op jit(solution)/shard_map/ppermute | solution.py:26
  23.8 1.7 %collective-permute-start.4 = (bf16[2,80,640]{2,1,0:T(8,128)(2,1)S(1)}, bf16[2,80,640]{2,1,0:T(8,128)(2,1)S(1)}, u32[]{:S(2)}, u32[]{:S(2)}) collective-permute-start(bf16[2,80,640]{2,1,0:T(8,128)(2,1)S(1)} %get-tuple-element.28.refs_3_), channel_id=1, source_target_pairs={{0,8},{2,10},{4,12},{6,14},{8,0},{10,2},{12,4},{14,6},{16,24},{18,... | collective-permute-start | bytes 614408 | tf_op jit(solution)/shard_map/ppermute | solution.py:26
  25.5 1.9 %collective-permute-done.5.refs_2_ = bf16[1,2,80,640]{3,2,1,0:T(8,128)(2,1)S(1)} collective-permute-done((bf16[1,2,80,640]{3,2,1,0:T(8,128)(2,1)S(1)}, bf16[1,2,80,640]{3,2,1,0:T(8,128)(2,1)S(1)}, u32[]{:S(2)}, u32[]{:S(2)}) %collective-permute-start.5) | collective-permute-done | bytes 204832 | tf_op jit(solution)/shard_map/ppermute | solution.py:26
  27.4 1.6 %collective-permute-start.7 = (bf16[1,80,640]{2,1,0:T(8,128)(2,1)S(1)}, bf16[1,80,640]{2,1,0:T(8,128)(2,1)S(1)}, u32[]{:S(2)}, u32[]{:S(2)}) collective-permute-start(bf16[1,80,640]{2,1,0:T(8,128)(2,1)S(1)} %get-tuple-element.31.refs_3_), channel_id=1, source_target_pairs={{0,8},{2,10},{4,12},{6,14},{8,0},{10,2},{12,4},{14,6},{16,24},{18,... | collective-permute-start | bytes 307208 | tf_op jit(solution)/shard_map/ppermute | solution.py:26
  29.1 2.7 %collective-permute-done.4.refs_2_ = bf16[2,80,640]{2,1,0:T(8,128)(2,1)S(1)} collective-permute-done((bf16[2,80,640]{2,1,0:T(8,128)(2,1)S(1)}, bf16[2,80,640]{2,1,0:T(8,128)(2,1)S(1)}, u32[]{:S(2)}, u32[]{:S(2)}) %collective-permute-start.4) | collective-permute-done | bytes 204832 | tf_op jit(solution)/shard_map/ppermute | solution.py:26
  31.8 0.7 %collective-permute-start.6 = (bf16[2,80,640]{2,1,0:T(8,128)(2,1)S(1)}, bf16[2,80,640]{2,1,0:T(8,128)(2,1)S(1)}, u32[]{:S(2)}, u32[]{:S(2)}) collective-permute-start(bf16[2,80,640]{2,1,0:T(8,128)(2,1)S(1)} %get-tuple-element.33.refs_3_.refs_4_), channel_id=1, source_target_pairs={{0,16},{2,18},{4,20},{6,22},{8,24},{10,26},{12,28},{14,30},{16,0},... | collective-permute-start | bytes 614408 | tf_op jit(solution)/shard_map/ppermute | solution.py:26
  32.6 1.6 %collective-permute-start.12 = (bf16[256,640]{1,0:T(8,128)(2,1)S(1)}, bf16[256,640]{1,0:T(8,128)(2,1)S(1)}, u32[]{:S(2)}, u32[]{:S(2)}) collective-permute-start(bf16[256,640]{1,0:T(8,128)(2,1)S(1)} %get-tuple-element.39), channel_id=1, source_target_pairs={{0,4},{2,6},{4,0},{6,2},{8,12},{10,14},{12,8},{14,10},{16,20},{18,... | collective-permute-start | bytes 983048 | tf_op jit(solution)/shard_map/ppermute | solution.py:26
  34.3 0.5 collective-permute-start.13
  34.8 2.3 %collective-permute-start.8 = (bf16[1,80,640]{2,1,0:T(8,128)(2,1)S(1)}, bf16[1,80,640]{2,1,0:T(8,128)(2,1)S(1)}, u32[]{:S(2)}, u32[]{:S(2)}) collective-permute-start(bf16[1,80,640]{2,1,0:T(8,128)(2,1)S(1)} %get-tuple-element.36), channel_id=1, source_target_pairs={{0,16},{2,18},{4,20},{6,22},{8,24},{10,26},{12,28},{14,30},{16,0},... | collective-permute-start | bytes 307208 | tf_op jit(solution)/shard_map/ppermute | solution.py:26
  37.1 8.9 %collective-permute-done.8.refs_5_ = bf16[1,80,640]{2,1,0:T(8,128)(2,1)S(1)} collective-permute-done((bf16[1,80,640]{2,1,0:T(8,128)(2,1)S(1)}, bf16[1,80,640]{2,1,0:T(8,128)(2,1)S(1)}, u32[]{:S(2)}, u32[]{:S(2)}) %collective-permute-start.8) | collective-permute-done | bytes 102432 | tf_op jit(solution)/shard_map/ppermute | solution.py:26
  46.4 1.6 %collective-permute-start.10 = (bf16[3,40,640]{2,1,0:T(8,128)(2,1)S(1)}, bf16[3,40,640]{2,1,0:T(8,128)(2,1)S(1)}, u32[]{:S(2)}, u32[]{:S(2)}) collective-permute-start(bf16[3,40,640]{2,1,0:T(8,128)(2,1)S(1)} %get-tuple-element.38.part_b), channel_id=1, source_target_pairs={{0,4},{2,6},{4,0},{6,2},{8,12},{10,14},{12,8},{14,10},{16,20},{18,... | collective-permute-start | bytes 460808 | tf_op jit(solution)/shard_map/ppermute | solution.py:26
  48.0 3.6 %collective-permute-done.9.got_a = bf16[3,40,640]{2,1,0:T(8,128)(2,1)S(1)} collective-permute-done((bf16[3,40,640]{2,1,0:T(8,128)(2,1)S(1)}, bf16[3,40,640]{2,1,0:T(8,128)(2,1)S(1)}, u32[]{:S(2)}, u32[]{:S(2)}) %collective-permute-start.9) | collective-permute-done | bytes 153632 | tf_op jit(solution)/shard_map/ppermute | solution.py:26
  51.9 0.5 collective-permute-start.17
  52.4 1.5 %collective-permute-start.14 = (bf16[3,80,640]{2,1,0:T(8,128)(2,1)S(1)}, bf16[3,80,640]{2,1,0:T(8,128)(2,1)S(1)}, u32[]{:S(2)}, u32[]{:S(2)}) collective-permute-start(bf16[3,80,640]{2,1,0:T(8,128)(2,1)S(1)} %get-tuple-element.41), channel_id=1, source_target_pairs={{0,4},{2,6},{4,0},{6,2},{8,12},{10,14},{12,8},{14,10},{16,20},{18,... | collective-permute-start | bytes 921608 | tf_op jit(solution)/shard_map/ppermute | solution.py:26
  53.9 1.9 %collective-permute-start.15 = (bf16[3,80,640]{2,1,0:T(8,128)(2,1)S(1)}, bf16[3,80,640]{2,1,0:T(8,128)(2,1)S(1)}, u32[]{:S(2)}, u32[]{:S(2)}) collective-permute-start(bf16[3,80,640]{2,1,0:T(8,128)(2,1)S(1)} %get-tuple-element.42), channel_id=1, source_target_pairs={{0,8},{2,10},{4,12},{6,14},{8,0},{10,2},{12,4},{14,6},{16,24},{18,... | collective-permute-start | bytes 921608 | tf_op jit(solution)/shard_map/ppermute | solution.py:26
  55.9 0.8 %first_half.1.half_out = f32[256,640]{1,0:T(8,128)S(1)} custom-call(bf16[256,640]{1,0:T(8,128)(2,1)S(1)} %copy-done.2, bf16[3,160,640]{2,1,0:T(8,128)(2,1)S(1)} %get-tuple-element.44.near, bf16[3,160,640]{2,1,0:T(8,128)(2,1)S(1)} %collective-permute-done.17.near_other), custom_call_target="tpu_custom_call" | custom-call | flops 314572800 | bytes 2457600 | tf_op jit(solution)/shard_map/first_half/pallas_call | solution.py:343
  56.8 4.7 %attention.1.attended = bf16[256,640]{1,0:T(8,128)(2,1)} custom-call(s32[1]{0:T(128)} %bitcast.place_ref.refs_0_, bf16[256,640]{1,0:T(8,128)(2,1)S(1)} %copy-done.6, bf16[256,640]{1,0:T(8,128)(2,1)S(1)} %copy-done, bf16[256,640]{1,0:T(8,128)(2,1)S(1)} %copy-done.1, bf16[256,640]{1,0:T(8,128)(2,1)S(1)} %collective-permute-done.12.back2_k, ...), custom_call_target="tpu_custom_call" | custom-call | flops 838860800 | bytes 3932160 | tf_op jit(solution)/shard_map/attention/pallas_call | solution.py:95
  61.7 1.4 %collective-permute-done.15.got_b = bf16[3,80,640]{2,1,0:T(8,128)(2,1)S(1)} collective-permute-done((bf16[3,80,640]{2,1,0:T(8,128)(2,1)S(1)}, bf16[3,80,640]{2,1,0:T(8,128)(2,1)S(1)}, u32[]{:S(2)}, u32[]{:S(2)}) %collective-permute-start.15) | collective-permute-done | bytes 307232 | tf_op jit(solution)/shard_map/ppermute | solution.py:26
  63.3 0.6 own_far.1.before
  63.9 1.4 %collective-permute-done.18.rows_ref = bf16[3,160,640]{2,1,0:T(8,128)(2,1)S(1)} collective-permute-done((bf16[3,160,640]{2,1,0:T(8,128)(2,1)S(1)}, bf16[3,160,640]{2,1,0:T(8,128)(2,1)S(1)}, u32[]{:S(2)}, u32[]{:S(2)}) %collective-permute-start.18) | collective-permute-done | bytes 614432 | tf_op jit(solution)/shard_map/ppermute | solution.py:26
  65.3 1.3 %last.1 = bf16[256,640]{1,0:T(8,128)(2,1)} custom-call(bf16[256,640]{1,0:T(8,128)(2,1)S(1)} %copy-done.2, f32[256,640]{1,0:T(8,128)S(1)} %own_far.1.before, bf16[3,160,640]{2,1,0:T(8,128)(2,1)S(1)} %collective-permute-done.18.rows_ref), custom_call_target="tpu_custom_call" | custom-call | flops 157286400 | bytes 614400 | tf_op jit(solution)/shard_map/last/pallas_call | solution.py:387
  (41 shorter events, 1.6 us)
Async XLA Ops:
  0.6 8.3 %collective-permute-start = (bf16[256,640]{1,0:T(8,128)(2,1)}, bf16[256,640]{1,0:T(8,128)(2,1)S(1)}, u32[]{:S(2)}, u32[]{:S(2)}) collective-permute-start(bf16[256,640]{1,0:T(8,128)(2,1)} %refs_2_.2), channel_id=1, source_target_pairs={{0,2},{2,0},{4,6},{6,4},{8,10},{10,8},{12,14},{14,12},{16,18},{18,... | collective-permute-start | bytes 983048 | tf_op jit(solution)/shard_map/ppermute | solution.py:26
  1.1 7.8 %collective-permute-start.1 = (bf16[256,640]{1,0:T(8,128)(2,1)}, bf16[256,640]{1,0:T(8,128)(2,1)S(1)}, u32[]{:S(2)}, u32[]{:S(2)}) collective-permute-start(bf16[256,640]{1,0:T(8,128)(2,1)} %refs_4_.1), channel_id=1, source_target_pairs={{0,2},{2,0},{4,6},{6,4},{8,10},{10,8},{12,14},{14,12},{16,18},{18,... | collective-permute-start | bytes 983048 | tf_op jit(solution)/shard_map/ppermute | solution.py:26
  1.2 4.5 %collective-permute-start.2 = (f32[256]{0:T(256)}, f32[256]{0:T(256)S(1)}, u32[]{:S(2)}, u32[]{:S(2)}) collective-permute-start(f32[256]{0:T(256)} %param.16), channel_id=1, source_target_pairs={{0,2},{2,0},{4,6},{6,4},{8,10},{10,8},{12,14},{14,12},{16,18},{18,... | collective-permute-start | bytes 3080 | tf_op jit(solution)/shard_map/ppermute | solution.py:26
  1.7 1.1 %copy-start.3 = (bf16[640,640]{1,0:T(8,128)(2,1)S(1)}, bf16[640,640]{1,0:T(8,128)(2,1)}, u32[]{:S(2)}) copy-start(bf16[640,640]{1,0:T(8,128)(2,1)} %gate_ref.1) | copy-start | bytes 2457604
  2.8 1.1 %copy-start.4 = (bf16[640,640]{1,0:T(8,128)(2,1)S(1)}, bf16[640,640]{1,0:T(8,128)(2,1)}, u32[]{:S(2)}) copy-start(bf16[640,640]{1,0:T(8,128)(2,1)} %up_ref.1) | copy-start | bytes 2457604
  4.0 1.1 %copy-start.5 = (bf16[640,640]{1,0:T(8,128)(2,1)S(1)}, bf16[640,640]{1,0:T(8,128)(2,1)}, u32[]{:S(2)}) copy-start(bf16[640,640]{1,0:T(8,128)(2,1)} %down_ref.1) | copy-start | bytes 2457604
  5.1 1.0 %copy-start = (bf16[256,640]{1,0:T(8,128)(2,1)S(1)}, bf16[256,640]{1,0:T(8,128)(2,1)}, u32[]{:S(2)}) copy-start(bf16[256,640]{1,0:T(8,128)(2,1)} %own_k.3) | copy-start | bytes 983044
  5.1 1.1 %copy-start.1 = (bf16[256,640]{1,0:T(8,128)(2,1)S(1)}, bf16[256,640]{1,0:T(8,128)(2,1)}, u32[]{:S(2)}) copy-start(bf16[256,640]{1,0:T(8,128)(2,1)} %own_v.3) | copy-start | bytes 983044
  5.7 3.3 %copy-start.7 = (bf16[256,640]{1,0:T(8,128)(2,1)S(1)}, bf16[256,640]{1,0:T(8,128)(2,1)}, u32[]{:S(2)}) copy-start(bf16[256,640]{1,0:T(8,128)(2,1)} %refs_2_.2) | copy-start | bytes 983044
  5.7 3.3 %copy-start.8 = (bf16[256,640]{1,0:T(8,128)(2,1)S(1)}, bf16[256,640]{1,0:T(8,128)(2,1)}, u32[]{:S(2)}) copy-start(bf16[256,640]{1,0:T(8,128)(2,1)} %refs_4_.1) | copy-start | bytes 983044
  5.7 3.3 %copy-start.9 = (f32[256]{0:T(256)S(1)}, f32[256]{0:T(256)}, u32[]{:S(2)}) copy-start(f32[256]{0:T(256)} %param.16) | copy-start | bytes 3076
  6.2 26.3 %collective-permute-start.11 = (bf16[2,256,640]{2,1,0:T(8,128)(2,1)S(1)}, bf16[2,256,640]{2,1,0:T(8,128)(2,1)S(1)}, u32[]{:S(2)}, u32[]{:S(2)}) collective-permute-start(bf16[2,256,640]{2,1,0:T(8,128)(2,1)S(1)} %pack.1.refs_8_), channel_id=1, source_target_pairs={{0,8},{2,10},{4,12},{6,14},{8,16},{10,18},{12,20},{14,22},{16,24},... | collective-permute-start | bytes 1966088 | tf_op jit(solution)/shard_map/ppermute | solution.py:410
  11.4 12.4 %collective-permute-start.3 = (bf16[2,2,80,640]{3,2,1,0:T(8,128)(2,1)S(1)}, bf16[2,2,80,640]{3,2,1,0:T(8,128)(2,1)S(1)}, u32[]{:S(2)}, u32[]{:S(2)}) collective-permute-start(bf16[2,2,80,640]{3,2,1,0:T(8,128)(2,1)S(1)} %get-tuple-element.26), channel_id=1, source_target_pairs={{0,4},{2,6},{4,0},{6,2},{8,12},{10,14},{12,8},{14,10},{16,20},{18,... | collective-permute-start | bytes 1228808 | tf_op jit(solution)/shard_map/ppermute | solution.py:26
  13.0 14.4 %collective-permute-start.5 = (bf16[1,2,80,640]{3,2,1,0:T(8,128)(2,1)S(1)}, bf16[1,2,80,640]{3,2,1,0:T(8,128)(2,1)S(1)}, u32[]{:S(2)}, u32[]{:S(2)}) collective-permute-start(bf16[1,2,80,640]{3,2,1,0:T(8,128)(2,1)S(1)} %get-tuple-element.30), channel_id=1, source_target_pairs={{0,4},{2,6},{4,0},{6,2},{8,12},{10,14},{12,8},{14,10},{16,20},{18,... | collective-permute-start | bytes 614408 | tf_op jit(solution)/shard_map/ppermute | solution.py:26
  23.8 7.9 %collective-permute-start.4 = (bf16[2,80,640]{2,1,0:T(8,128)(2,1)S(1)}, bf16[2,80,640]{2,1,0:T(8,128)(2,1)S(1)}, u32[]{:S(2)}, u32[]{:S(2)}) collective-permute-start(bf16[2,80,640]{2,1,0:T(8,128)(2,1)S(1)} %get-tuple-element.28.refs_3_), channel_id=1, source_target_pairs={{0,8},{2,10},{4,12},{6,14},{8,0},{10,2},{12,4},{14,6},{16,24},{18,... | collective-permute-start | bytes 614408 | tf_op jit(solution)/shard_map/ppermute | solution.py:26
  27.4 7.3 %collective-permute-start.7 = (bf16[1,80,640]{2,1,0:T(8,128)(2,1)S(1)}, bf16[1,80,640]{2,1,0:T(8,128)(2,1)S(1)}, u32[]{:S(2)}, u32[]{:S(2)}) collective-permute-start(bf16[1,80,640]{2,1,0:T(8,128)(2,1)S(1)} %get-tuple-element.31.refs_3_), channel_id=1, source_target_pairs={{0,8},{2,10},{4,12},{6,14},{8,0},{10,2},{12,4},{14,6},{16,24},{18,... | collective-permute-start | bytes 307208 | tf_op jit(solution)/shard_map/ppermute | solution.py:26
  31.8 14.1 %collective-permute-start.6 = (bf16[2,80,640]{2,1,0:T(8,128)(2,1)S(1)}, bf16[2,80,640]{2,1,0:T(8,128)(2,1)S(1)}, u32[]{:S(2)}, u32[]{:S(2)}) collective-permute-start(bf16[2,80,640]{2,1,0:T(8,128)(2,1)S(1)} %get-tuple-element.33.refs_3_.refs_4_), channel_id=1, source_target_pairs={{0,16},{2,18},{4,20},{6,22},{8,24},{10,26},{12,28},{14,30},{16,0},... | collective-permute-start | bytes 614408 | tf_op jit(solution)/shard_map/ppermute | solution.py:26
  32.6 15.3 %collective-permute-start.12 = (bf16[256,640]{1,0:T(8,128)(2,1)S(1)}, bf16[256,640]{1,0:T(8,128)(2,1)S(1)}, u32[]{:S(2)}, u32[]{:S(2)}) collective-permute-start(bf16[256,640]{1,0:T(8,128)(2,1)S(1)} %get-tuple-element.39), channel_id=1, source_target_pairs={{0,4},{2,6},{4,0},{6,2},{8,12},{10,14},{12,8},{14,10},{16,20},{18,... | collective-permute-start | bytes 983048 | tf_op jit(solution)/shard_map/ppermute | solution.py:26
  34.3 13.7 %collective-permute-start.13 = (bf16[256,640]{1,0:T(8,128)(2,1)S(1)}, bf16[256,640]{1,0:T(8,128)(2,1)S(1)}, u32[]{:S(2)}, u32[]{:S(2)}) collective-permute-start(bf16[256,640]{1,0:T(8,128)(2,1)S(1)} %get-tuple-element.40), channel_id=1, source_target_pairs={{0,4},{2,6},{4,0},{6,2},{8,12},{10,14},{12,8},{14,10},{16,20},{18,... | collective-permute-start | bytes 983048 | tf_op jit(solution)/shard_map/ppermute | solution.py:26
  34.8 11.2 %collective-permute-start.8 = (bf16[1,80,640]{2,1,0:T(8,128)(2,1)S(1)}, bf16[1,80,640]{2,1,0:T(8,128)(2,1)S(1)}, u32[]{:S(2)}, u32[]{:S(2)}) collective-permute-start(bf16[1,80,640]{2,1,0:T(8,128)(2,1)S(1)} %get-tuple-element.36), channel_id=1, source_target_pairs={{0,16},{2,18},{4,20},{6,22},{8,24},{10,26},{12,28},{14,30},{16,0},... | collective-permute-start | bytes 307208 | tf_op jit(solution)/shard_map/ppermute | solution.py:26
  46.3 9.6 %copy-start.2 = (bf16[256,640]{1,0:T(8,128)(2,1)S(1)}, bf16[256,640]{1,0:T(8,128)(2,1)}, u32[]{:S(2)}) copy-start(bf16[256,640]{1,0:T(8,128)(2,1)} %q_ref.7) | copy-start | bytes 983044
  46.3 5.3 %collective-permute-start.9 = (bf16[3,40,640]{2,1,0:T(8,128)(2,1)S(1)}, bf16[3,40,640]{2,1,0:T(8,128)(2,1)S(1)}, u32[]{:S(2)}, u32[]{:S(2)}) collective-permute-start(bf16[3,40,640]{2,1,0:T(8,128)(2,1)S(1)} %get-tuple-element.37.part_a), channel_id=1, source_target_pairs={{0,8},{2,10},{4,12},{6,14},{8,0},{10,2},{12,4},{14,6},{16,24},{18,... | collective-permute-start | bytes 460808 | tf_op jit(solution)/shard_map/ppermute | solution.py:26
  46.4 5.3 %collective-permute-start.10 = (bf16[3,40,640]{2,1,0:T(8,128)(2,1)S(1)}, bf16[3,40,640]{2,1,0:T(8,128)(2,1)S(1)}, u32[]{:S(2)}, u32[]{:S(2)}) collective-permute-start(bf16[3,40,640]{2,1,0:T(8,128)(2,1)S(1)} %get-tuple-element.38.part_b), channel_id=1, source_target_pairs={{0,4},{2,6},{4,0},{6,2},{8,12},{10,14},{12,8},{14,10},{16,20},{18,... | collective-permute-start | bytes 460808 | tf_op jit(solution)/shard_map/ppermute | solution.py:26
  51.8 4.9 %copy-start.6 = (bf16[256,640]{1,0:T(8,128)(2,1)S(1)}, bf16[256,640]{1,0:T(8,128)(2,1)}, u32[]{:S(2)}) copy-start(bf16[256,640]{1,0:T(8,128)(2,1)} %q_ref.4) | copy-start | bytes 983044
  51.8 4.9 %collective-permute-start.16 = (bf16[2,2,256,640]{3,2,1,0:T(8,128)(2,1)S(1)}, bf16[2,2,256,640]{3,2,1,0:T(8,128)(2,1)S(1)}, u32[]{:S(2)}, u32[]{:S(2)}) collective-permute-start(bf16[2,2,256,640]{3,2,1,0:T(8,128)(2,1)S(1)} %get-tuple-element.43), channel_id=1, source_target_pairs={{0,2},{2,0},{4,6},{6,4},{8,10},{10,8},{12,14},{14,12},{16,18},{18,... | collective-permute-start | bytes 3932168 | tf_op jit(solution)/shard_map/ppermute | solution.py:26
  51.9 4.0 %collective-permute-start.17 = (bf16[3,160,640]{2,1,0:T(8,128)(2,1)S(1)}, bf16[3,160,640]{2,1,0:T(8,128)(2,1)S(1)}, u32[]{:S(2)}, u32[]{:S(2)}) collective-permute-start(bf16[3,160,640]{2,1,0:T(8,128)(2,1)S(1)} %get-tuple-element.44.near), channel_id=1, source_target_pairs={{0,2},{2,0},{4,6},{6,4},{8,10},{10,8},{12,14},{14,12},{16,18},{18,... | collective-permute-start | bytes 1843208 | tf_op jit(solution)/shard_map/ppermute | solution.py:26
  52.4 9.3 %collective-permute-start.14 = (bf16[3,80,640]{2,1,0:T(8,128)(2,1)S(1)}, bf16[3,80,640]{2,1,0:T(8,128)(2,1)S(1)}, u32[]{:S(2)}, u32[]{:S(2)}) collective-permute-start(bf16[3,80,640]{2,1,0:T(8,128)(2,1)S(1)} %get-tuple-element.41), channel_id=1, source_target_pairs={{0,4},{2,6},{4,0},{6,2},{8,12},{10,14},{12,8},{14,10},{16,20},{18,... | collective-permute-start | bytes 921608 | tf_op jit(solution)/shard_map/ppermute | solution.py:26
  53.9 9.2 %collective-permute-start.15 = (bf16[3,80,640]{2,1,0:T(8,128)(2,1)S(1)}, bf16[3,80,640]{2,1,0:T(8,128)(2,1)S(1)}, u32[]{:S(2)}, u32[]{:S(2)}) collective-permute-start(bf16[3,80,640]{2,1,0:T(8,128)(2,1)S(1)} %get-tuple-element.42), channel_id=1, source_target_pairs={{0,8},{2,10},{4,12},{6,14},{8,0},{10,2},{12,4},{14,6},{16,24},{18,... | collective-permute-start | bytes 921608 | tf_op jit(solution)/shard_map/ppermute | solution.py:26
  63.2 2.1 %collective-permute-start.18 = (bf16[3,160,640]{2,1,0:T(8,128)(2,1)S(1)}, bf16[3,160,640]{2,1,0:T(8,128)(2,1)S(1)}, u32[]{:S(2)}, u32[]{:S(2)}) collective-permute-start(bf16[3,160,640]{2,1,0:T(8,128)(2,1)S(1)} %get-tuple-element.47.rows_ref), channel_id=1, source_target_pairs={{0,2},{2,0},{4,6},{6,4},{8,10},{10,8},{12,14},{14,12},{16,18},{18,... | collective-permute-start | bytes 1843208 | tf_op jit(solution)/shard_map/ppermute | solution.py:26
